TPU v7x, 256 devices: a whole 4x4x8 slice. The times are simulated.
256 devices in a mesh: row: 32 (over z, y), col: 8 (over x, core).
Axes of the slice: x: 4, y: 4, z: 8, core: 2. Of those that a mesh axis runs over, the one named last changes fastest.
Arguments:
- tokens: bfloat16 [1024, 12288], P('row', 'col'), may hold values from -6 to 6
- w_in: bfloat16 [12288, 24576], P('col', 'row'), may hold values from -0.0546875 to 0.0546875
- bias_in: float32 [24576], P('row'), may hold values from -4 to 4
- w_out: bfloat16 [24576, 12288], P('row', 'col'), may hold values from -0.0390625 to 0.0390625
- bias_out: float32 [12288], P('col'), may hold values from -4 to 4
- cotangent: bfloat16 [1024, 12288], P('row', 'col'), may hold values from -6 to 6
Outputs:
- outputs: bfloat16 [1024, 12288], P('row', 'col')
- d_tokens: bfloat16 [1024, 12288], P('row', 'col')
- grad_w_in: bfloat16 [12288, 24576], P('col', 'row')
- grad_bias_in: float32 [24576], P('row')
- grad_w_out: bfloat16 [24576, 12288], P('row', 'col')
- grad_bias_out: float32 [12288], P('col')
All inputs are finite; a program needn't handle non-finite values.
Results may differ from a plain program's by a relative error of at most 0.03.
Values may be sent and summed in bfloat16 or wider, within the bound.
A program may use at most 64 MiB of HBM per device.

v0:
```python
import math

import jax
import jax.numpy as jnp
from jax import lax
from jax.sharding import PartitionSpec as P

gelu_coef = math.sqrt(2.0 / math.pi)


def gelu_pair(preact):
    inner = gelu_coef * (preact + 0.044715 * preact * preact * preact)
    tangent = jnp.tanh(inner)
    value = 0.5 * preact * (1.0 + tangent)
    slope = 0.5 * (1.0 + tangent) + 0.5 * preact * (1.0 - tangent * tangent) * gelu_coef * (
        1.0 + 3.0 * 0.044715 * preact * preact
    )
    return (value, slope)


def contract(left, right, left_dim, right_dim):
    return lax.dot_general(
        left, right, (((left_dim,), (right_dim,)), ((), ())), preferred_element_type=jnp.float32
    )


def body(tokens, w_in, bias_in, w_out, bias_out, cotangent):
    tok_all, cot_all = (
        lax.all_gather(tokens, "row", axis=0, tiled=True),
        lax.all_gather(cotangent, "row", axis=0, tiled=True),
    )
    preact = (
        lax.psum(
            jnp.dot(tok_all, w_in, preferred_element_type=jnp.float32).astype(jnp.bfloat16), "col"
        ).astype(jnp.float32)
        + bias_in
    )
    value, slope = gelu_pair(preact)
    hidden = value.astype(jnp.bfloat16)
    block = hidden
    outputs = (
        lax.psum_scatter(
            jnp.dot(block, w_out, preferred_element_type=jnp.float32).astype(jnp.bfloat16),
            "row",
            scatter_dimension=0,
            tiled=True,
        ).astype(jnp.float32)
        + bias_out
    ).astype(jnp.bfloat16)
    d_hidden = lax.psum(contract(cot_all, w_out, 1, 1).astype(jnp.bfloat16), "col").astype(
        jnp.float32
    )
    d_preact = (d_hidden * slope).astype(jnp.bfloat16)
    grad_w_out = contract(hidden, cot_all, 0, 0).astype(jnp.bfloat16)
    grad_bias_out = jnp.sum(cot_all.astype(jnp.float32), axis=0)
    grad_w_in = contract(tok_all, d_preact, 0, 0).astype(jnp.bfloat16)
    grad_bias_in = jnp.sum(d_preact.astype(jnp.float32), axis=0)
    block = d_preact
    d_tokens = lax.psum_scatter(
        contract(block, w_in, 1, 1).astype(jnp.bfloat16), "row", scatter_dimension=0, tiled=True
    )
    return (outputs, d_tokens, grad_w_in, grad_bias_in, grad_w_out, grad_bias_out)


def solution(mesh):
    return jax.shard_map(
        body,
        mesh=mesh,
        in_specs=(
            P("row", "col"),
            P("col", "row"),
            P("row"),
            P("row", "col"),
            P("col"),
            P("row", "col"),
        ),
        out_specs=(
            P("row", "col"),
            P("row", "col"),
            P("col", "row"),
            P("row"),
            P("row", "col"),
            P("col"),
        ),
        check_vma=False,
    )
```

profile of v0, /device:TPU:32, one launch (start us, length us, event | category | flops | bytes accessed | tf_op | source)
XLA Modules:
  0.0 704.3 jit_solution(14515568403956065893)
XLA Ops:
  7.2 0.0 copy-start
  7.2 0.0 all-gather.5.cloned.1.call-start
  7.2 0.7 all-gather.5.cloned.1.call-update
  7.9 0.0 all-gather.3.cloned.1.call-start
  8.0 0.7 all-gather.3.cloned.1.call-update
  8.7 0.0 all-reduce.3.cloned.1.call-start
  8.7 83.7 %all-gather.5.cloned.1.call-done = bf16[1024,1536]{1,0:T(8,128)(2,1)} async-done(((bf16[32,1536]{1,0:T(8,128)(2,1)}), bf16[1024,1536]{1,0:T(8,128)(2,1)}) %all-gather.5.cloned.1.call-update) | async-done | bytes 3145744 | tf_op jit(solution)/shard_map/all_gather | solution.py:30
  92.4 0.0 copy-done
  92.4 5.7 convolution_convert_fusion.4
  98.1 73.5 %all-gather.3.cloned.1.call-done = bf16[1024,1536]{1,0:T(8,128)(2,1)} async-done(((bf16[32,1536]{1,0:T(8,128)(2,1)}), bf16[1024,1536]{1,0:T(8,128)(2,1)}) %all-gather.3.cloned.1.call-update) | async-done | bytes 3145744 | tf_op jit(solution)/shard_map/all_gather | solution.py:29
  171.6 6.4 convolution_convert_fusion.5
  178.0 0.0 copy-start.4
  178.0 0.0 all-reduce.3.cloned.1.call-update
  178.0 0.0 reduce-scatter.3.cloned.1.call-start
  178.1 71.7 %all-reduce.3.cloned.1.call-done = (bf16[1024,768]{1,0:T(8,128)(2,1)}, bf16[1024,768]{1,0:T(8,128)(2,1)}) async-done(((bf16[1024,768]{1,0:T(8,128)(2,1)}, bf16[1024,768]{1,0:T(8,128)(2,1)}), (bf16[1024,768]{1,0:T(8,128)(2,1)}, bf16[1024,768]{1,0:T(8,128)(2,1)})) %all-reduce.3.cloned.1.call-update) | async-done | bytes 3145744 | tf_op jit(solution)/shard_map/psum | solution.py:33
  249.8 0.0 copy-done.4
  249.8 7.0 %convolution_convert_fusion.1 = bf16[1024,1536]{1,0:T(8,128)(2,1)} fusion(bf16[768,1536]{1,0:T(8,128)(2,1)S(1)} %copy-done, bf16[1024,768]{1,0:T(8,128)(2,1)} %get-tuple-element.12, f32[768]{0:T(1024)S(1)} %copy-done.4), kind=kOutput, calls=%fused_computation.4 | convolution fusion | flops 2426142720 | bytes 7080960 | tf_op jit(solution)/shard_map/dot_general | solution.py:43
  256.8 0.0 reduce-scatter.3.cloned.1.call-update
  256.9 0.2 reduce-scatter.5.cloned.1.call-start
  257.1 0.0 copy-start.5
  257.1 4.6 convert_reduce_fusion.1
  261.7 0.0 copy-start.1
  261.7 1.1 copy-done.1
  262.8 0.0 copy-done.5
  262.8 4.1 convolution_convert_fusion
  266.9 0.0 reduce-scatter.5.cloned.1.call-update
  266.9 0.0 copy-start.2
  266.9 3.1 convert_reduce_fusion
  270.0 0.0 copy-done.2
  270.0 5.8 fusion.9
  275.8 4.3 copy.12
  280.0 0.0 copy-start.3
  280.0 6.9 convolution_convert_fusion.2
  287.0 188.4 %reduce-scatter.3.cloned.1.call-done = bf16[32,1536]{1,0:T(8,128)(2,1)} async-done(((bf16[1024,1536]{1,0:T(8,128)(2,1)}), bf16[32,1536]{1,0:T(8,128)(2,1)}) %reduce-scatter.3.cloned.1.call-update) | async-done | bytes 98320 | tf_op jit(solution)/shard_map/reduce_scatter | solution.py:42
  475.3 0.0 copy-done.3
  475.3 1.6 add_convert_fusion
  476.9 220.9 %reduce-scatter.5.cloned.1.call-done = bf16[32,1536]{1,0:T(8,128)(2,1)} async-done(((bf16[1024,1536]{1,0:T(8,128)(2,1)}), bf16[32,1536]{1,0:T(8,128)(2,1)}) %reduce-scatter.5.cloned.1.call-update) | async-done | bytes 98320 | tf_op jit(solution)/shard_map/reduce_scatter | solution.py:59
Async XLA Ops:
  7.2 85.3 %copy-start = (bf16[768,1536]{1,0:T(8,128)(2,1)S(1)}, bf16[768,1536]{1,0:T(8,128)(2,1)}, u32[]{:S(2)}) copy-start(bf16[768,1536]{1,0:T(8,128)(2,1)} %param.9) | copy-start | bytes 7077892
  7.2 85.3 %all-gather.5.cloned.1.call-start = ((), (), s32[]{:S(2)}) async-start(), calls=%async_computation.4 | async-start | bytes 3244032 | tf_op jit(solution)/shard_map/all_gather | solution.py:30
  7.9 163.7 %all-gather.3.cloned.1.call-start = ((), (), s32[]{:S(2)}) async-start(), calls=%async_computation.2 | async-start | bytes 3244032 | tf_op jit(solution)/shard_map/all_gather | solution.py:29
  8.7 241.1 %all-reduce.3.cloned.1.call-start = ((), (), s32[]{:S(2)}) async-start(), calls=%async_computation.6 | async-start | bytes 6291456 | tf_op jit(solution)/shard_map/psum | solution.py:33
  178.0 71.8 %copy-start.4 = (f32[768]{0:T(1024)S(1)}, f32[768]{0:T(1024)}, u32[]{:S(2)}) copy-start(f32[768]{0:T(1024)} %param.8) | copy-start | bytes 9220
  178.0 297.3 %reduce-scatter.3.cloned.1.call-start = ((), (), s32[]{:S(2)}) async-start(), calls=%async_computation.3 | async-start | bytes 3244032 | tf_op jit(solution)/shard_map/reduce_scatter | solution.py:42
  256.9 440.9 %reduce-scatter.5.cloned.1.call-start = ((), (), s32[]{:S(2)}) async-start(), calls=%async_computation.5 | async-start | bytes 3244032 | tf_op jit(solution)/shard_map/reduce_scatter | solution.py:59
  257.1 5.7 copy-start.5
  261.7 1.1 copy-start.1
  266.9 3.1 copy-start.2
  280.0 195.3 %copy-start.3 = (f32[1536]{0:T(1024)S(1)}, f32[1536]{0:T(1024)}, u32[]{:S(2)}) copy-start(f32[1536]{0:T(1024)} %param.10) | copy-start | bytes 18436
Sparse Core Ops, SparseCore 0:
  10.6 81.8 all-gather.4
  95.0 76.5 all-gather.2
  178.1 71.6 all-reduce.2
  257.0 218.3 reduce-scatter.2
  480.1 217.6 reduce-scatter.4
where the time goes:
time: 706 us; the launch traced here: 704 us
  waiting for transfers between devices  640 us (91%)
  matrix products  35.8 us (5%)
  between operations  13.8 us (2%)
  other arithmetic  9.22 us (1%)
    reduce_scatter x1, waiting for transfers between devices, body(): lax.psum_scatter(contract(block, w_in, 1, 1).astype(jnp.bfloat16), 'row',...  221 us
    reduce_scatter x1, waiting for transfers between devices, body(): lax.psum_scatter(jnp.dot(block, w_out, preferred_element_type=jnp.float32...  188 us
    all_gather x1, waiting for transfers between devices, body(): lax.all_gather(cotangent, 'row', axis=0, tiled=True)  83.7 us
    all_gather x1, waiting for transfers between devices, body(): lax.all_gather(tokens, 'row', axis=0, tiled=True)  73.5 us
    psum x1, waiting for transfers between devices, body(): lax.psum(jnp.dot(tok_all, w_in, preferred_element_type=jnp.float32).astyp...  71.7 us
    dot_general x4, matrix products, contract(): lax.dot_general(left, right, (((left_dim,), (right_dim,)), ((), ())), pre...  22.4 us
  transfers between devices with their start and end apart: 5, of which 5 were waited for; matrix products, arithmetic and copies ran while one was open for 5% of the time, Pallas kernels for 0%

commit v1 on v0

v1 whole, which is shorter than its diff:
```python
import math
from types import SimpleNamespace

import jax
import jax.numpy as jnp
from jax import lax
from jax.experimental import pallas as pl
from jax.experimental.pallas import tpu as pltpu
from jax.sharding import PartitionSpec as P

MESH = pl.DeviceIdType.MESH
BF, F32 = jnp.bfloat16, jnp.float32
NZ, NY, NX = 8, 4, 4
SHARD, DW, FW = 32, 1536, 768
CHUNK = 64
CA = 640
CB = DW - CA
POS = (0, 1, 4, 5, 7, 6, 3, 2)
SLOT = (0, 1, 7, 6, 2, 3, 5, 4)
ARRIVAL = (0, 1, 7, 2, 6, 3, 5, 4)
ZP, ZM, YP, YM, XP, XM, ZP2, ZM2, Y2, X2, CORE, LOCAL = range(12)
LINKS = ((ZP,), (ZM,), (YP,), (YM,), (XP,), (XM,), (ZP, ZP), (ZM, ZM), (YP, YM), (XP, XM), (), ())
QUICK, BRIEF, DIRECT = (True, False), (True, True), (True, True)
RATE, RATE_CORE, RATE_LOCAL = 44000.0, 600e3, 2.5e6
HOP, HOP_CORE, EACH = 2.6, 1.5, 0.03
RANK = (0.2, 0.2, 0.2, 0, 0.3, 0.3, 0.3, 0.3, 1.0, 0.665, 0.7, 0.045, 2.409, 0.627, 1.7, 1.61, 2.842, 2.7, 2.091, 2.7, 2.69, 4.014, 3.491, 5.647, 5.352, 5.527, 7.485, 9)
AHEAD = (1.5, 1.5, 1.5, 0.5, 0.0, 0.0, 0.0, 1.5, 2, 1.0, 5, 0.0, 0.5, 0.5, 0.5, 0.5, 0.2, 0.5, 0.5, 0.5, 1.5, 0.2, 1.0, 1.0, 1.0, 0.2, 0.2, 1)
EPS = 0.2
HALVES = ((0, 1), (0, 1))
gelu_coef = math.sqrt(2.0 / math.pi)


def gelu_pair(preact):
    inner = gelu_coef * (preact + 0.044715 * preact * preact * preact)
    tangent = jnp.tanh(inner)
    value = 0.5 * preact * (1.0 + tangent)
    slope = 0.5 * (1.0 + tangent) + 0.5 * preact * (1.0 - tangent * tangent) * gelu_coef * (
        1.0 + 3.0 * 0.044715 * preact * preact
    )
    return value, slope


def contract(left, right, left_dim, right_dim):
    return lax.dot_general(
        left, right, (((left_dim,), (right_dim,)), ((), ())), preferred_element_type=F32
    )


class Copy:
    def __init__(self, way, src, dst, size, land=None):
        self.way, self.src, self.dst, self.size = way, src, dst, size
        self.land = land or dst
        self.index = self.due = None
        self.then = []


class Task:
    def __init__(self, group, needs=(), after=(), run=None, cost=0.01, starts=(), minor=0.0):
        self.prio, self.ahead, self.group = RANK[group] + minor, AHEAD[group], group
        self.needs, self.after = list(needs), list(after)
        self.run, self.cost, self.starts = run, cost, list(starts)
        self.then = []


def arrange(tasks, log=None):
    now, free, order, left = 0.0, [0.0] * 12, [], list(tasks)
    for t in left:
        t.wait = len(set(t.after)) + len(set(t.needs))
        for one in set(t.after) | set(t.needs):
            one.then.append(t)
    able = [t for t in left if t.wait == 0]
    while able:
        best = None
        for place, t in enumerate(able):
            ready = max([now] + [n.due for n in t.needs])
            for c in t.starts:
                for link in LINKS[c.way]:
                    ready = max(ready, free[link] - t.ahead)
            key = (0.0 if ready <= now + EPS else ready, t.prio, place)
            if best is None or key < best[0]:
                best = (key, t)
        t = best[1]
        able.remove(t)
        begin = max([now] + [n.due for n in t.needs])
        if log is not None:
            log.append((begin, begin - now, t))
        now = begin + t.cost + EACH
        for c in t.starts:
            now += EACH
            if c.way >= CORE:
                free[c.way] = max(now, free[c.way]) + c.size / (RATE_CORE if c.way == CORE else RATE_LOCAL)
                c.due = free[c.way] + HOP_CORE
                continue
            c.due = 0.0
            for link in LINKS[c.way]:
                free[link] = max(now, free[link]) + c.size / RATE
                c.due = max(c.due, free[link] + HOP + (0.5 if c.way >= ZP2 else 0.0))
        order.append(t)
        for one in [t] + t.starts:
            for later in one.then:
                later.wait -= 1
                if later.wait == 0:
                    able.append(later)
    return order


def plan(r, at):
    copies, tasks = [], []

    def copy(way, src, dst, size, land=None):
        c = Copy(way, src, dst, size, land)
        c.index = len(copies)
        copies.append(c)
        return c

    def task(*args, **kw):
        t = Task(*args, **kw)
        tasks.append(t)
        return t

    def send(group, needs, way, src, dst, size, land=None, **kw):
        c = copy(way, src, dst, size, land)
        task(group, needs, starts=[c], **kw)
        return c

    A, B = slice(0, CA), slice(CA, DW)
    full, lo, hi = slice(0, SHARD), slice(0, 16), slice(16, 32)
    szA, szB = SHARD * CA * 2, SHARD * CB * 2

    def gather(arg, buf, quick, base):
        def ref(slot, *index):
            return lambda: buf().at[(POS[slot],) + index]

        def own(cols):
            return lambda: arg().at[:, cols]

        load = copy(LOCAL, arg, ref(0, 0), SHARD * DW * 2)
        whole = [[] for _ in range(NZ)]
        whole[0].append(load)
        yp0 = send(base, [], YP, own(A), ref(0, 2, full, A), szA)
        ym0 = send(base, [], YM, own(A), ref(0, 1, full, A), szA)
        zp = [send(base + 2, [], ZP, own(B), ref(7, 0, full, B), szB)]
        zm = [send(base + 2, [], ZM, own(B), ref(1, 0, full, B), szB)]
        task(base, starts=[load])
        y2 = send(base, [], Y2, own(A), ref(0, 3, full, A), szA)
        whole[0] += [yp0, ym0, y2]
        for s, need in enumerate(([], [ym0], [yp0], [y2])):
            for way in (ZP, ZM):
                got = need
                for k in range(4):
                    if k == 3 and (s < 2) != (way == ZP):
                        continue
                    here, there = ((8 - k) % 8, 7 - k) if way == ZP else (k, k + 1)
                    src = own(A) if k == 0 and s == 0 else ref(here, s, full, A)
                    got = [send(base + 1, got, way, src, ref(there, s, full, A), szA, minor=0.001 * k)]
                    whole[there] += got
        if quick:
            zp.append(send(base + 2, [], ZP2, own(B), ref(6, 0, full, B), szB))
            zm.append(send(base + 2, [], ZM2, own(B), ref(2, 0, full, B), szB))
            zp.append(send(base + 2, zp[1:], ZP, ref(6, 0, full, B), ref(5, 0, full, B), szB))
            zm.append(send(base + 2, zm[1:], ZM, ref(2, 0, full, B), ref(3, 0, full, B), szB))
            zp.append(send(base + 2, zp[1:2], ZP2, ref(6, 0, lo, B), ref(4, 0, lo, B), szB // 2))
            zm.append(send(base + 2, zm[1:2], ZM2, ref(2, 0, hi, B), ref(4, 0, hi, B), szB // 2))
        for k in range(1, 1 if quick else 4):
            rows, size = (lo, szB // 2) if k == 3 else (full, szB)
            zp.append(send(base + 2, zp[-1:], ZP, ref(8 - k, 0, rows, B), ref(7 - k, 0, rows, B), size))
            rows = hi if k == 3 else full
            zm.append(send(base + 2, zm[-1:], ZM, ref(k, 0, rows, B), ref(k + 1, 0, rows, B), size))
        column = [[load], zm[:1], zm[1:2], zm[2:3], [zp[3], zm[3]], zp[2:3], zp[1:2], zp[:1]]
        for i, slot in enumerate(ARRIVAL):
            src = own(B) if slot == 0 else ref(slot, 0, full, B)
            need = [] if slot == 0 else column[slot]
            p = send(base + 3, need, YP, src, ref(slot, 2, full, B), szB, minor=0.001 * i)
            m = send(base + 3, need, YM, src, ref(slot, 1, full, B), szB, minor=0.001 * i)
            if i % 2 == 0:
                last = send(base + 3, [p], YP, ref(slot, 2, full, B), ref(slot, 3, full, B), szB, minor=0.001 * i - 0.002)
            else:
                last = send(base + 3, [m], YM, ref(slot, 1, full, B), ref(slot, 3, full, B), szB, minor=0.001 * i - 0.002)
            whole[slot] += [p, m, last] + [c for c in column[slot] if c is not load]
        return whole

    tok = gather(lambda: r.tokens, lambda: r.T, QUICK[0], 0)
    load_in = copy(LOCAL, lambda: r.w_in, lambda: r.WI, DW * FW * 2)
    load_out = copy(LOCAL, lambda: r.w_out, lambda: r.WO, DW * FW * 2)
    load_bias_in = copy(LOCAL, lambda: r.bias_in, lambda: r.BI.at[0], FW * 4)
    load_bias_out = copy(LOCAL, lambda: r.bias_out, lambda: r.BO.at[0], DW * 4)
    task(0, starts=[load_in, load_out, load_bias_in, load_bias_out])
    cot = gather(lambda: r.cotangent, lambda: r.C, QUICK[1], 4)

    def reduce_col(buf, whole, weight, load, dim, s, total, finish, also, halves, direct, base):
        lo, hi = slice(0, 32), slice(32, 64)
        piece = 32 * FW * 2
        swaps = []

        def product(q, n):
            def run():
                left = buf()[2 * q : 2 * q + 2].reshape(256, DW)
                cols = slice(n * 256, n * 256 + 256)
                value = contract(left, weight()[:, cols], 1, 0) if dim == 0 else contract(left, weight()[cols, :], 1, 1)
                s().part[2 * q : 2 * q + 2, :, :, cols] = value.astype(BF).reshape(2, 2, CHUNK, 256)

            return run

        for q in [2 * h + i for h in halves for i in (0, 1)]:
            need = whole[SLOT[2 * q]] + whole[SLOT[2 * q + 1]] + [load]
            made = [task(base, need, run=product(q, n), cost=0.215) for n in range(3)]
            planes = slice(2 * q, 2 * q + 2)
            swaps.append(
                send(base + 1, [], CORE, lambda planes=planes: s().part.at[planes, at.other],
                     lambda planes=planes: s().swap.at[planes], 4 * piece, after=made)
            )
        ready = [None, None]
        for turn, h in enumerate(halves):
            swapped = swaps[2 * turn : 2 * turn + 2]

            def plane(rel, h=h):
                return 4 * h + at.x[rel]

            def add(rel, rows, extra=None, plane=plane, h=h):
                def run():
                    i = plane(rel)
                    value = s().part[i, at.core, rows, :].astype(F32) + s().swap[i, rows, :].astype(F32)
                    if extra is not None:
                        value = value + s().first[h, extra].astype(F32)
                    s().part[i, at.core, rows, :] = value.astype(BF)

                return run

            def part(rel, rows, plane=plane):
                return lambda: s().part.at[plane(rel), at.core, rows]

            def first(d, h=h):
                return lambda: s().first.at[h, d]

            def second(d, rows, h=h):
                return lambda: s().second.at[h, d, rows]

            u, v = base + 1, dict(minor=0.01 * turn)
            if direct:
                both = slice(0, CHUNK)
                p1 = send(u, swapped, XP, part(1, both), second(0, both), 2 * piece, run=add(1, both), cost=0.02, **v)
                m1 = send(u, swapped, XM, part(3, both), second(1, both), 2 * piece, run=add(3, both), cost=0.02, **v)
                p2 = m2 = send(u, swapped, X2, part(2, both), second(2, both), 2 * piece, run=add(2, both), cost=0.02, **v)
            else:
                p0 = send(u, swapped, XP, part(2, lo), first(0), piece, run=add(2, lo), cost=0.02, **v)
                m0 = send(u, swapped, XM, part(2, hi), first(1), piece, run=add(2, hi), cost=0.02, **v)
                p1 = send(u, swapped, XP, part(1, hi), second(0, hi), piece, run=add(1, hi), cost=0.02, **v)
                m1 = send(u, swapped, XM, part(3, lo), second(1, lo), piece, run=add(3, lo), cost=0.02, **v)
                p2 = send(u, swapped + [p0], XP, part(1, lo), second(0, lo), piece, run=add(1, lo, 0), cost=0.02, **v)
                m2 = send(u, swapped + [m0], XM, part(3, hi), second(1, hi), piece, run=add(3, hi, 1), cost=0.02, **v)

            def out(rel, core, rows, plane=plane):
                return lambda: total().at[plane(rel), getattr(at, core), rows]

            def final(at_row, plane=plane, h=h):
                def run():
                    @pl.loop(0, 2)
                    def _(n):
                        rows = pl.ds(pl.multiple_of(at_row + n * 16, 16), 16)
                        i = plane(0)
                        value = s().part[i, at.core, rows, :].astype(F32) + s().swap[i, rows, :].astype(F32)
                        for d in range(3 if direct else 2):
                            value = value + s().second[h, d, rows, :].astype(F32)
                        total()[i, at.core, rows, :] = finish(value, h, rows)

                return run

            me, ot = "core", "other"
            done, moved = [], {}
            for need, rows, at_row in (([p1, m2], hi, 32), ([p2, m1], lo, 0)):
                cp = copy(XP, out(0, me, rows), out(0, me, rows), piece, out(3, me, rows))
                cm = copy(XM, out(0, me, rows), out(0, me, rows), piece, out(1, me, rows))
                cs = copy(CORE, out(0, me, rows), out(0, me, rows), piece, out(0, ot, rows))
                starts = [cp, cm, cs]
                if direct:
                    need = [p1, m1, p2]
                    moved[2, at_row] = copy(X2, out(0, me, rows), out(0, me, rows), piece, out(2, me, rows))
                    starts.append(moved[2, at_row])
                task(base + 2, swapped + need + also, run=final(at_row), cost=0.17, starts=starts, **v)
                moved[3, at_row], moved[1, at_row] = cp, cm
                done.append(cs)
            for rel in (3, 1, 2) if direct else (3, 1):
                for rows, at_row in ((lo, 0), (hi, 32)):
                    c = moved[rel, at_row]
                    done += [c, send(base + 3, [c], CORE, out(rel, me, rows), out(rel, me, rows), piece, out(rel, ot, rows), **v)]
            for way, rel, rows, at_row in () if direct else ((XP, 3, lo, 0), (XM, 1, hi, 32)):
                c = send(base + 2, [moved[rel, at_row]], way, out(rel, me, rows), out(rel, me, rows), piece, out(2, me, rows), **v)
                done += [c, send(base + 3, [c], CORE, out(2, me, rows), out(2, me, rows), piece, out(2, ot, rows), **v)]
            ready[h] = done
        return ready

    def finish_hidden(value, h, rows):
        value, slope = gelu_pair(value + r.BI[...])
        r.slope[h, rows, :] = slope
        return value.astype(BF)

    def finish_d(value, h, rows):
        return (value * r.slope[h, rows, :]).astype(BF)

    hidden = reduce_col(
        lambda: r.T, tok, lambda: r.WI, load_in, 0, lambda: r.sum_h, lambda: r.H, finish_hidden, [load_bias_in], HALVES[0], DIRECT[0], 8)
    d_preact = reduce_col(
        lambda: r.C, cot, lambda: r.WO, load_out, 1, lambda: r.sum_d, lambda: r.D, finish_d, [], HALVES[1], DIRECT[1], 12)

    def reduce_row(total, ready, weight, dim, s, bias, also, target, brief, base):
        def product(q, n):
            def run():
                left = total()[2 * q : 2 * q + 2].reshape(256, FW)
                cols = slice(n * 512, n * 512 + 512)
                value = contract(left, weight()[:, cols], 1, 0) if dim == 0 else contract(left, weight()[cols, :], 1, 1)
                s().part[2 * q : 2 * q + 2, :, :, cols] = value.astype(BF).reshape(2, NY, SHARD, 512)

            return run

        made = {}
        for q in (0, 1, 3, 2):
            for n in range(3):
                made[q, n] = task(base, ready[q // 2], run=product(q, n), cost=0.215, minor=0.001 * n)

        def have(slot, cols):
            q = POS[slot] // 2
            return [made[q, n] for n in ((0, 1) if cols is A else (1, 2))]

        def ref(slot, *index):
            return lambda: s().part.at[(POS[slot],) + index]

        def add(slot, index, *sources):
            def run():
                place = (POS[slot],) + index
                value = s().part[place].astype(F32)
                for pick, at_place in sources:
                    value = value + pick(s())[at_place].astype(F32)
                s().part[place] = value.astype(BF)

            return run

        za, ya, yb, zb = (lambda t: t.za), (lambda t: t.ya), (lambda t: t.yb), (lambda t: t.zb)

        def buf(pick, *index):
            return lambda: pick(s()).at[index]

        own, got = {}, {}
        for s_ in (3, 1, 2, 0):
            ends = []
            for d, way in ((0, ZP), (1, ZM)):
                prev = None
                for k in range(4):
                    if k == 0 and (s_ < 2) != (way == ZP):
                        continue
                    slot = 4 - k if way == ZP else (4 + k) % 8
                    run = None if prev is None else add(slot, (s_, full, A), (za, (d, k - 1, s_)))
                    prev = send(base + 1, [prev] if prev else [], way, ref(slot, s_, full, A), buf(za, d, k, s_),
                                szA, minor=0.001 * (4 - k), after=have(slot, A), run=run, cost=0.02 if run else 0.01)
                ends.append(prev)
            own[s_] = task(base + 1, ends, have(0, A), run=add(0, (s_, full, A), (za, (0, 3, s_)), (za, (1, 3, s_))), cost=0.02)
        y2 = send(base + 2, [], Y2, ref(0, 3, full, A), buf(ya, 2), szA, after=[own[3]])
        p1 = send(base + 2, [], YP, ref(0, 1, full, A), buf(ya, 0), szA, after=[own[1]])
        m1 = send(base + 2, [], YM, ref(0, 2, full, A), buf(ya, 1), szA, after=[own[2]])
        summed = {}
        for i, slot in enumerate(reversed(ARRIVAL)):
            z = POS[slot]
            v = dict(minor=0.001 * i)
            d = i % 2
            here = have(slot, B)
            c0 = send(base + 3, [], (YP, YM)[d], ref(slot, 3, full, B), buf(yb, d, 0, z), szB, after=here, **v)
            ends = []
            for e, way in ((0, YP), (1, YM)):
                run = add(slot, (1 + e, full, B), (yb, (e, 0, z))) if e == d else None
                ends.append(send(base + 3, [c0] if run else [], way, ref(slot, 1 + e, full, B), buf(yb, e, 1, z), szB,
                                 after=here, run=run, cost=0.025 if run else 0.01, **v))
            summed[slot] = task(base + 3, ends, here, run=add(slot, (0, full, B), (yb, (0, 1, z)), (yb, (1, 1, z))), cost=0.03, **v)
        ends = []
        for d, way, way2 in ((0, ZP, ZP2), (1, ZM, ZM2)):
            prev = None
            half = (lo, hi)[d]
            if brief:
                far, near, mid, end = (4, 3, 2, 1) if way == ZP else (4, 5, 6, 7)
                b = base + 4
                c0 = send(b, [], way2, ref(far, 0, half, B), buf(zb, d, 0, half), szB // 2, after=[summed[far]])
                c1 = send(b, [], way, ref(near, 0, full, B), buf(zb, d, 1), szB, after=[summed[near]])
                c3 = send(b, [], way, ref(end, 0, full, B), buf(zb, d, 3), szB, after=[summed[end]])
                join = task(b, [c0, c1], [summed[mid]], run=add(mid, (0, full, B), (zb, (d, 1))), cost=0.02)
                c2 = send(b, [c0, c1], way2, ref(mid, 0, full, B), buf(zb, d, 2), szB, after=[join],
                          run=add(mid, (0, half, B), (zb, (d, 0, half))), cost=0.02)
                ends += [c2, c3]
                continue
            for k in range(4):
                slot = 4 - k if way == ZP else (4 + k) % 8
                rows, rows_in = (half if k == 0 else full), (half if k == 1 else full)
                run = None if prev is None else add(slot, (0, rows_in, B), (zb, (d, k - 1, rows_in)))
                prev = send(base + 4, [prev] if prev else [], way, ref(slot, 0, rows, B), buf(zb, d, k, rows),
                            szB // 2 if k == 0 else szB, after=[summed[slot]], run=run, cost=0.02 if run else 0.03)
            ends.append(prev)

        def last(cols, pick, places):
            def run():
                value = s().part[0, 0, :, cols].astype(F32)
                for place in places:
                    value = value + pick(s())[place].astype(F32)
                if bias is not None:
                    value = value + bias()[:, cols]
                target()[:, cols] = value.astype(BF)

            return run

        task(base + 2, [p1, m1, y2] + also, [own[0]], run=last(A, ya, (0, 1, 2)), cost=0.03)
        task(base + 4, ends + also, [summed[0]], run=last(B, zb, ((0, 3), (1, 3), (0, 2), (1, 2)) if brief else ((0, 3), (1, 3))), cost=0.03)

    reduce_row(lambda: r.H, hidden, lambda: r.WO, 0, lambda: r.sum_o, lambda: r.BO, [load_bias_out], lambda: r.outputs, BRIEF[0], 16)
    reduce_row(lambda: r.D, d_preact, lambda: r.WI, 1, lambda: r.sum_t, None, [], lambda: r.d_tokens, BRIEF[1], 21)

    all_tok, all_cot = sum(tok, []), sum(cot, [])

    def grad(left, right, target, i, wide):
        def run():
            cols = slice(i * 256, i * 256 + 256)
            a = left()[..., cols].reshape(1024, 256)
            target()[cols, :] = contract(a, right()[...].reshape(1024, wide), 0, 0).astype(BF)

        return run

    def column_sum(source, target):
        def run():
            whole = source()
            lead, width = whole.shape[1], whole.shape[-1]

            def step(n, total):
                return total + whole[n // lead, lax.rem(n, lead)].astype(F32)

            total = lax.fori_loop(0, NZ * lead, step, jnp.zeros(whole.shape[2:], F32))
            target()[...] = jnp.sum(total, axis=0, keepdims=True)

        return run

    for i in range(3):
        task(26, all_cot + sum(hidden, []), run=grad(lambda: r.H, lambda: r.C, lambda: r.grad_w_out, i, DW), cost=0.95)
    for i in range(6):
        task(26, all_tok + sum(d_preact, []), run=grad(lambda: r.T, lambda: r.D, lambda: r.grad_w_in, i, FW), cost=0.45)
    task(27, all_cot, run=column_sum(lambda: r.C, lambda: r.grad_bias_out), cost=0.75)
    task(27, sum(d_preact, []), run=column_sum(lambda: r.D, lambda: r.grad_bias_in), cost=0.4)
    return copies, tasks


def buffers():
    def v(*shape, dtype=BF):
        return pltpu.VMEM(shape, dtype)

    def col():
        return dict(part=v(NZ, 2, CHUNK, FW), swap=v(NZ, CHUNK, FW), first=v(2, 2, 32, FW), second=v(2, 3, CHUNK, FW))

    def row():
        return dict(part=v(NZ, NY, SHARD, DW), za=v(2, 4, NY, SHARD, CA), ya=v(3, SHARD, CA),
                    yb=v(2, 2, NZ, SHARD, CB), zb=v(2, 4, SHARD, CB))

    return dict(
        T=v(NZ, NY, SHARD, DW), C=v(NZ, NY, SHARD, DW), WI=v(DW, FW), WO=v(FW, DW),
        H=v(NZ, 2, CHUNK, FW), D=v(NZ, 2, CHUNK, FW), slope=v(2, CHUNK, FW, dtype=F32), BI=v(1, FW, dtype=F32), BO=v(1, DW, dtype=F32),
        sum_h=col(), sum_d=col(), sum_o=row(), sum_t=row(),
    )


def kernel(tokens, w_in, bias_in, w_out, bias_out, cotangent,
           outputs, d_tokens, grad_w_in, grad_bias_in, grad_w_out, grad_bias_out, scratch, send, recv):
    r = SimpleNamespace(**{k: SimpleNamespace(**b) if isinstance(b, dict) else b for k, b in scratch.items()})
    r.tokens, r.w_in, r.bias_in, r.w_out, r.bias_out, r.cotangent = tokens, w_in, bias_in, w_out, bias_out, cotangent
    r.outputs, r.d_tokens, r.grad_w_in, r.grad_bias_in = outputs, d_tokens, grad_w_in, grad_bias_in
    r.grad_w_out, r.grad_bias_out = grad_w_out, grad_bias_out
    row, col = lax.axis_index("row"), lax.axis_index("col")
    z, y, x, core = row // NY, lax.rem(row, NY), col // 2, lax.rem(col, 2)
    other = 1 - core
    xs = (x,) + tuple(lax.rem(x + d, NX) for d in (1, 2, 3))
    at = SimpleNamespace(x=xs, core=core, other=other)
    to = (
        (lax.rem(z + 1, NZ) * NY + y, col), (lax.rem(z + NZ - 1, NZ) * NY + y, col),
        (z * NY + lax.rem(y + 1, NY), col), (z * NY + lax.rem(y + NY - 1, NY), col),
        (row, xs[1] * 2 + core), (row, xs[3] * 2 + core),
        (lax.rem(z + 2, NZ) * NY + y, col), (lax.rem(z + NZ - 2, NZ) * NY + y, col),
        (z * NY + lax.rem(y + 2, NY), col), (row, xs[2] * 2 + core), (row, x * 2 + other),
    )
    barrier = pltpu.get_barrier_semaphore()
    for target in to:
        pl.semaphore_signal(barrier, inc=1, device_id=target, device_id_type=MESH)
    pl.semaphore_wait(barrier, len(to))

    def describe(c, dst):
        if c.way == LOCAL:
            return pltpu.make_async_copy(c.src(), dst(), recv.at[c.index])
        return pltpu.make_async_remote_copy(
            src_ref=c.src(), dst_ref=dst(), send_sem=send.at[c.index], recv_sem=recv.at[c.index],
            device_id=to[c.way], device_id_type=MESH,
        )

    copies, tasks = plan(r, at)
    waited = set()
    for t in arrange(tasks):
        for c in t.needs:
            if c.index not in waited:
                waited.add(c.index)
                if c.way == LOCAL:
                    describe(c, c.dst).wait()
                else:
                    describe(c, c.land).wait_recv()
        if t.run is not None:
            t.run()
        for c in t.starts:
            describe(c, c.dst).start()
    for c in copies:
        if c.way != LOCAL:
            describe(c, c.dst).wait_send()


def store_kernel(*refs):
    count = (len(refs) - 1) // 2
    moves = [
        pltpu.make_async_copy(refs[i] if len(refs[count + i].shape) == 2 else refs[i].at[0], refs[count + i], refs[-1].at[i])
        for i in range(count)
    ]
    for move in moves:
        move.start()
    for move in moves:
        move.wait()


def body(tokens, w_in, bias_in, w_out, bias_out, cotangent):
    any_space = pl.BlockSpec(memory_space=pl.ANY)
    vmem = pl.BlockSpec(memory_space=pltpu.VMEM)
    count = len(plan(None, None)[0])
    shapes = (((SHARD, DW), BF), ((SHARD, DW), BF), ((DW, FW), BF), ((1, FW), F32), ((FW, DW), BF), ((1, DW), F32))
    results = pl.pallas_call(
        kernel,
        out_shape=tuple(pltpu.VMEM(shape, dtype) for shape, dtype in shapes),
        in_specs=[any_space] * 6,
        out_specs=(vmem,) * 6,
        scratch_shapes=[buffers(), pltpu.SemaphoreType.DMA((count,)), pltpu.SemaphoreType.DMA((count,))],
        compiler_params=pltpu.CompilerParams(
            collective_id=0, has_side_effects=True, vmem_limit_bytes=52 << 20
        ),
        cost_estimate=pl.CostEstimate(
            flops=6 * 2 * 1024 * DW * FW, bytes_accessed=8 * DW * FW, transcendentals=128 * FW
        ),
        name="ffn",
    )(tokens, w_in, bias_in, w_out, bias_out, cotangent)
    results = pl.pallas_call(
        store_kernel,
        out_shape=tuple(jax.ShapeDtypeStruct(shape if shape[0] > 1 else shape[1:], dtype) for shape, dtype in shapes),
        in_specs=[any_space] * 6,
        out_specs=(any_space,) * 6,
        scratch_shapes=[pltpu.SemaphoreType.DMA((6,))],
        compiler_params=pltpu.CompilerParams(vmem_limit_bytes=1 << 20),
        name="store",
    )(*results)
    outputs, d_tokens, grad_w_in, grad_bias_in, grad_w_out, grad_bias_out = results
    return (outputs, d_tokens, grad_w_in, grad_bias_in, grad_w_out, grad_bias_out)


def solution(mesh):
    return jax.shard_map(
        body,
        mesh=mesh,
        in_specs=(
            P("row", "col"),
            P("col", "row"),
            P("row"),
            P("row", "col"),
            P("col"),
            P("row", "col"),
        ),
        out_specs=(
            P("row", "col"),
            P("row", "col"),
            P("col", "row"),
            P("row"),
            P("row", "col"),
            P("col"),
        ),
        check_vma=False,
    )
```

time: 706 us -> 111 us (0.16)
  waiting for transfers between devices: 640 us -> 0 us
  Pallas kernels: 0 us -> 110 us
  matrix products: 35.8 us -> 0 us
  between operations: 13.8 us -> 0.8 us
  other arithmetic: 9.22 us -> 0 us
    reduce_scatter x2 -> x0, waiting for transfers between devices: 409 us -> none  [the longest x1 221 us: body(): lax.psum_scatter(contract(block, w_in, 1, 1).astype(jnp.bfloat16), 'row',...]
    all_gather x2 -> x0, waiting for transfers between devices: 157 us -> none  [the longest x1 83.7 us: body(): lax.all_gather(cotangent, 'row', axis=0, tiled=True)]
    pallas_call x0 -> x2, Pallas kernels: none -> 110 us  [the longest x1 108 us: body(): pl.pallas_call(kernel, out_shape=tuple((pltpu.VMEM(shape, dtype) for shap...]
    psum x1 -> x0, waiting for transfers between devices: 71.7 us -> none  [body(): lax.psum(jnp.dot(tok_all, w_in, preferred_element_type=jnp.float32).astyp...]
    dot_general x6 -> x0, matrix products: 35.8 us -> none  [the longest x4 22.4 us: contract(): lax.dot_general(left, right, (((left_dim,), (right_dim,)), ((), ())), pre...]
    reduce_sum x2 -> x0, other arithmetic: 7.67 us -> none  [the longest x1 4.57 us: body(): grad_bias_in = jnp.sum(d_preact.astype(jnp.float32), axis=0)]
  transfers between devices with their start and end apart: 5 -> 0, of which waited for: 5 -> 0; matrix products, arithmetic and copies ran while one was open for 5% -> 0% of each run, Pallas kernels for 0% -> 0%
where the time goes in v1:
time: 111 us
  Pallas kernels  110 us (99%)
    pallas_call x1, Pallas kernels, body(): pl.pallas_call(kernel, out_shape=tuple((pltpu.VMEM(shape, dtype) for shap...  108 us
    pallas_call x1, Pallas kernels, body(): pl.pallas_call(store_kernel, out_shape=tuple((jax.ShapeDtypeStruct(shape...  2.31 us

profile of v1, /device:TPU:32, one launch (start us, length us, event | category | flops | bytes accessed | tf_op | source)
XLA Modules:
  0.0 110.9 jit_solution(6684217483199660816)
XLA Ops:
  0.6 107.8 %ffn.1 = (bf16[32,1536]{1,0:T(8,128)(2,1)S(1)}, bf16[32,1536]{1,0:T(8,128)(2,1)S(1)}, bf16[1536,768]{1,0:T(8,128)(2,1)S(1)}, f32[1,768]{1,0:T(1,128)S(1)}, bf16[...) custom-call(bf16[32,1536]{1,0:T(8,128)(2,1)} %tokens.1, bf16[1536,768]{1,0:T(8,128)(2,1)} %w_in.1, f32[768]{0:T(1024)} %bias_in.1, ...), custom_call_target="tpu_custom_call" | custom-call | flops 14495514624 | bytes 9437184 | tf_op jit(solution)/shard_map/ffn/pallas_call | solution.py:529
  108.4 2.3 %store.1 = (bf16[32,1536]{1,0:T(8,128)(2,1)}, bf16[32,1536]{1,0:T(8,128)(2,1)}, bf16[1536,768]{1,0:T(8,128)(2,1)}, f32[768]{0:T(1024)}, bf16[768,1536]{1,0:T(8,128)(2,1)}, /*index=5*/f32[1536]{0:T(1024)}) custom-call(bf16[32,1536]{1,0:T(8,128)(2,1)S(1)} %get-tuple-element.12.refs_0_, bf16[32,1536]{1,0:T(8,128)(2,1)S(1)} %get-tuple-element.13.refs_1_, ...), custom_call_target="tpu_custom_call" | custom-call | tf_op jit(solution)/shard_map/store/pallas_call | solution.py:543

commit v2 on v1

--- a/solution.py
+++ b/solution.py
@@ -18,15 +18,27 @@
 POS = (0, 1, 4, 5, 7, 6, 3, 2)
 SLOT = (0, 1, 7, 6, 2, 3, 5, 4)
 ARRIVAL = (0, 1, 7, 2, 6, 3, 5, 4)
-ZP, ZM, YP, YM, XP, XM, ZP2, ZM2, Y2, X2, CORE, LOCAL = range(12)
-LINKS = ((ZP,), (ZM,), (YP,), (YM,), (XP,), (XM,), (ZP, ZP), (ZM, ZM), (YP, YM), (XP, XM), (), ())
-QUICK, BRIEF, DIRECT = (True, False), (True, True), (True, True)
-RATE, RATE_CORE, RATE_LOCAL = 44000.0, 600e3, 2.5e6
-HOP, HOP_CORE, EACH = 2.6, 1.5, 0.03
-RANK = (0.2, 0.2, 0.2, 0, 0.3, 0.3, 0.3, 0.3, 1.0, 0.665, 0.7, 0.045, 2.409, 0.627, 1.7, 1.61, 2.842, 2.7, 2.091, 2.7, 2.69, 4.014, 3.491, 5.647, 5.352, 5.527, 7.485, 9)
-AHEAD = (1.5, 1.5, 1.5, 0.5, 0.0, 0.0, 0.0, 1.5, 2, 1.0, 5, 0.0, 0.5, 0.5, 0.5, 0.5, 0.2, 0.5, 0.5, 0.5, 1.5, 0.2, 1.0, 1.0, 1.0, 0.2, 0.2, 1)
-EPS = 0.2
+ZP, ZM, YP, YM, XP, XM, CORE, LOCAL = range(8)
 HALVES = ((0, 1), (0, 1))
+ORDER = (2, 3, 0, 1, 67, 66, 68, 69, 11, 7, 41, 42, 24, 35, 36, 6, 5, 18, 14, 45, 47, 48, 102, 44, 21, 8, 111, 31,
+    72, 37, 43, 65, 38, 25, 4, 12, 28, 46, 15, 50, 19, 53, 101, 51, 49, 117, 32, 71, 9, 39, 59, 54, 40, 22, 131, 57,
+    26, 29, 56, 16, 104, 55, 103, 132, 52, 13, 63, 33, 133, 134, 10, 62, 90, 107, 58, 80, 61, 23, 60, 30, 20, 27, 17,
+    64, 73, 123, 113, 34, 137, 136, 97, 119, 125, 122, 77, 135, 138, 116, 106, 94, 105, 141, 87, 126, 81, 118, 84,
+    139, 148, 150, 140, 142, 147, 144, 143, 145, 146, 98, 74, 91, 114, 120, 149, 95, 164, 129, 163, 78, 70, 124, 166,
+    88, 151, 85, 115, 165, 82, 121, 128, 99, 152, 75, 110, 92, 127, 168, 79, 96, 167, 89, 86, 154, 109, 83, 100, 130,
+    183, 76, 93, 169, 108, 184, 112, 185, 186, 170, 153, 159, 188, 189, 187, 190, 155, 193, 192, 191, 194, 177, 175,
+    212, 172, 211, 180, 181, 171, 161, 174, 179, 182, 214, 158, 160, 173, 156, 157, 213, 178, 176, 216, 196, 215,
+    233, 234, 263, 242, 235, 275, 251, 247, 195, 277, 162, 258, 236, 237, 255, 238, 283, 239, 279, 267, 293, 217,
+    291, 232, 218, 264, 197, 243, 231, 287, 200, 276, 248, 230, 252, 198, 229, 199, 256, 259, 285, 284, 225, 240,
+    228, 268, 296, 281, 223, 265, 244, 303, 304, 227, 280, 278, 311, 307, 253, 201, 289, 288, 249, 257, 220, 202,
+    292, 260, 219, 301, 221, 286, 222, 226, 224, 266, 269, 241, 295, 245, 323, 324, 337, 332, 325, 365, 348, 341,
+    353, 369, 204, 209, 328, 207, 327, 373, 250, 326, 381, 357, 375, 329, 290, 367, 305, 203, 206, 409, 345, 419,
+    333, 338, 294, 366, 261, 210, 308, 205, 246, 349, 354, 208, 370, 254, 371, 330, 282, 312, 374, 321, 322, 377,
+    385, 320, 334, 299, 346, 378, 271, 318, 319, 270, 368, 401, 397, 389, 339, 342, 350, 272, 393, 358, 383, 262,
+    410, 317, 382, 355, 416, 386, 331, 379, 297, 376, 335, 414, 372, 402, 398, 300, 420, 387, 347, 407, 309, 313,
+    343, 412, 418, 411, 351, 340, 336, 362, 361, 391, 390, 384, 399, 380, 403, 421, 274, 359, 356, 395, 394, 298,
+    314, 413, 302, 310, 344, 417, 352, 273, 363, 364, 388, 392, 400, 404, 415, 360, 315, 408, 306, 405, 316, 396,
+    406)
 gelu_coef = math.sqrt(2.0 / math.pi)
 
 
@@ -56,52 +68,8 @@
 
 class Task:
     def __init__(self, group, needs=(), after=(), run=None, cost=0.01, starts=(), minor=0.0):
-        self.prio, self.ahead, self.group = RANK[group] + minor, AHEAD[group], group
-        self.needs, self.after = list(needs), list(after)
-        self.run, self.cost, self.starts = run, cost, list(starts)
-        self.then = []
-
-
-def arrange(tasks, log=None):
-    now, free, order, left = 0.0, [0.0] * 12, [], list(tasks)
-    for t in left:
-        t.wait = len(set(t.after)) + len(set(t.needs))
-        for one in set(t.after) | set(t.needs):
-            one.then.append(t)
-    able = [t for t in left if t.wait == 0]
-    while able:
-        best = None
-        for place, t in enumerate(able):
-            ready = max([now] + [n.due for n in t.needs])
-            for c in t.starts:
-                for link in LINKS[c.way]:
-                    ready = max(ready, free[link] - t.ahead)
-            key = (0.0 if ready <= now + EPS else ready, t.prio, place)
-            if best is None or key < best[0]:
-                best = (key, t)
-        t = best[1]
-        able.remove(t)
-        begin = max([now] + [n.due for n in t.needs])
-        if log is not None:
-            log.append((begin, begin - now, t))
-        now = begin + t.cost + EACH
-        for c in t.starts:
-            now += EACH
-            if c.way >= CORE:
-                free[c.way] = max(now, free[c.way]) + c.size / (RATE_CORE if c.way == CORE else RATE_LOCAL)
-                c.due = free[c.way] + HOP_CORE
-                continue
-            c.due = 0.0
-            for link in LINKS[c.way]:
-                free[link] = max(now, free[link]) + c.size / RATE
-                c.due = max(c.due, free[link] + HOP + (0.5 if c.way >= ZP2 else 0.0))
-        order.append(t)
-        for one in [t] + t.starts:
-            for later in one.then:
-                later.wait -= 1
-                if later.wait == 0:
-                    able.append(later)
-    return order
+        self.group, self.cost, self.minor = group, cost, minor
+        self.needs, self.after, self.run, self.starts = list(needs), list(after), run, list(starts)
 
 
 def plan(r, at):
@@ -127,7 +95,7 @@
     full, lo, hi = slice(0, SHARD), slice(0, 16), slice(16, 32)
     szA, szB = SHARD * CA * 2, SHARD * CB * 2
 
-    def gather(arg, buf, quick, base):
+    def gather(arg, buf, base):
         def ref(slot, *index):
             return lambda: buf().at[(POS[slot],) + index]
 
@@ -142,9 +110,10 @@
         zp = [send(base + 2, [], ZP, own(B), ref(7, 0, full, B), szB)]
         zm = [send(base + 2, [], ZM, own(B), ref(1, 0, full, B), szB)]
         task(base, starts=[load])
-        y2 = send(base, [], Y2, own(A), ref(0, 3, full, A), szA)
-        whole[0] += [yp0, ym0, y2]
-        for s, need in enumerate(([], [ym0], [yp0], [y2])):
+        yp1 = send(base, [yp0], YP, ref(0, 2, lo, A), ref(0, 3, lo, A), szA // 2)
+        ym1 = send(base, [ym0], YM, ref(0, 1, hi, A), ref(0, 3, hi, A), szA // 2)
+        whole[0] += [yp0, ym0, yp1, ym1]
+        for s, need in enumerate(([], [ym0], [yp0], [yp1, ym1])):
             for way in (ZP, ZM):
                 got = need
                 for k in range(4):
@@ -154,14 +123,7 @@
                     src = own(A) if k == 0 and s == 0 else ref(here, s, full, A)
                     got = [send(base + 1, got, way, src, ref(there, s, full, A), szA, minor=0.001 * k)]
                     whole[there] += got
-        if quick:
-            zp.append(send(base + 2, [], ZP2, own(B), ref(6, 0, full, B), szB))
-            zm.append(send(base + 2, [], ZM2, own(B), ref(2, 0, full, B), szB))
-            zp.append(send(base + 2, zp[1:], ZP, ref(6, 0, full, B), ref(5, 0, full, B), szB))
-            zm.append(send(base + 2, zm[1:], ZM, ref(2, 0, full, B), ref(3, 0, full, B), szB))
-            zp.append(send(base + 2, zp[1:2], ZP2, ref(6, 0, lo, B), ref(4, 0, lo, B), szB // 2))
-            zm.append(send(base + 2, zm[1:2], ZM2, ref(2, 0, hi, B), ref(4, 0, hi, B), szB // 2))
-        for k in range(1, 1 if quick else 4):
+        for k in range(1, 4):
             rows, size = (lo, szB // 2) if k == 3 else (full, szB)
             zp.append(send(base + 2, zp[-1:], ZP, ref(8 - k, 0, rows, B), ref(7 - k, 0, rows, B), size))
             rows = hi if k == 3 else full
@@ -179,15 +141,15 @@
             whole[slot] += [p, m, last] + [c for c in column[slot] if c is not load]
         return whole
 
-    tok = gather(lambda: r.tokens, lambda: r.T, QUICK[0], 0)
+    tok = gather(lambda: r.tokens, lambda: r.T, 0)
     load_in = copy(LOCAL, lambda: r.w_in, lambda: r.WI, DW * FW * 2)
     load_out = copy(LOCAL, lambda: r.w_out, lambda: r.WO, DW * FW * 2)
     load_bias_in = copy(LOCAL, lambda: r.bias_in, lambda: r.BI.at[0], FW * 4)
     load_bias_out = copy(LOCAL, lambda: r.bias_out, lambda: r.BO.at[0], DW * 4)
     task(0, starts=[load_in, load_out, load_bias_in, load_bias_out])
-    cot = gather(lambda: r.cotangent, lambda: r.C, QUICK[1], 4)
-
-    def reduce_col(buf, whole, weight, load, dim, s, total, finish, also, halves, direct, base):
+    cot = gather(lambda: r.cotangent, lambda: r.C, 4)
+
+    def reduce_col(buf, whole, weight, load, dim, s, total, finish, also, halves, base):
         lo, hi = slice(0, 32), slice(32, 64)
         piece = 32 * FW * 2
         swaps = []
@@ -236,18 +198,12 @@
                 return lambda: s().second.at[h, d, rows]
 
             u, v = base + 1, dict(minor=0.01 * turn)
-            if direct:
-                both = slice(0, CHUNK)
-                p1 = send(u, swapped, XP, part(1, both), second(0, both), 2 * piece, run=add(1, both), cost=0.02, **v)
-                m1 = send(u, swapped, XM, part(3, both), second(1, both), 2 * piece, run=add(3, both), cost=0.02, **v)
-                p2 = m2 = send(u, swapped, X2, part(2, both), second(2, both), 2 * piece, run=add(2, both), cost=0.02, **v)
-            else:
-                p0 = send(u, swapped, XP, part(2, lo), first(0), piece, run=add(2, lo), cost=0.02, **v)
-                m0 = send(u, swapped, XM, part(2, hi), first(1), piece, run=add(2, hi), cost=0.02, **v)
-                p1 = send(u, swapped, XP, part(1, hi), second(0, hi), piece, run=add(1, hi), cost=0.02, **v)
-                m1 = send(u, swapped, XM, part(3, lo), second(1, lo), piece, run=add(3, lo), cost=0.02, **v)
-                p2 = send(u, swapped + [p0], XP, part(1, lo), second(0, lo), piece, run=add(1, lo, 0), cost=0.02, **v)
-                m2 = send(u, swapped + [m0], XM, part(3, hi), second(1, hi), piece, run=add(3, hi, 1), cost=0.02, **v)
+            p0 = send(u, swapped, XP, part(2, lo), first(0), piece, run=add(2, lo), cost=0.02, **v)
+            m0 = send(u, swapped, XM, part(2, hi), first(1), piece, run=add(2, hi), cost=0.02, **v)
+            p1 = send(u, swapped, XP, part(1, hi), second(0, hi), piece, run=add(1, hi), cost=0.02, **v)
+            m1 = send(u, swapped, XM, part(3, lo), second(1, lo), piece, run=add(3, lo), cost=0.02, **v)
+            p2 = send(u, swapped + [p0], XP, part(1, lo), second(0, lo), piece, run=add(1, lo, 0), cost=0.02, **v)
+            m2 = send(u, swapped + [m0], XM, part(3, hi), second(1, hi), piece, run=add(3, hi, 1), cost=0.02, **v)
 
             def out(rel, core, rows, plane=plane):
                 return lambda: total().at[plane(rel), getattr(at, core), rows]
@@ -259,7 +215,7 @@
                         rows = pl.ds(pl.multiple_of(at_row + n * 16, 16), 16)
                         i = plane(0)
                         value = s().part[i, at.core, rows, :].astype(F32) + s().swap[i, rows, :].astype(F32)
-                        for d in range(3 if direct else 2):
+                        for d in range(2):
                             value = value + s().second[h, d, rows, :].astype(F32)
                         total()[i, at.core, rows, :] = finish(value, h, rows)
 
@@ -271,19 +227,14 @@
                 cp = copy(XP, out(0, me, rows), out(0, me, rows), piece, out(3, me, rows))
                 cm = copy(XM, out(0, me, rows), out(0, me, rows), piece, out(1, me, rows))
                 cs = copy(CORE, out(0, me, rows), out(0, me, rows), piece, out(0, ot, rows))
-                starts = [cp, cm, cs]
-                if direct:
-                    need = [p1, m1, p2]
-                    moved[2, at_row] = copy(X2, out(0, me, rows), out(0, me, rows), piece, out(2, me, rows))
-                    starts.append(moved[2, at_row])
-                task(base + 2, swapped + need + also, run=final(at_row), cost=0.17, starts=starts, **v)
+                task(base + 2, swapped + need + also, run=final(at_row), cost=0.17, starts=[cp, cm, cs], **v)
                 moved[3, at_row], moved[1, at_row] = cp, cm
                 done.append(cs)
-            for rel in (3, 1, 2) if direct else (3, 1):
+            for rel in (3, 1):
                 for rows, at_row in ((lo, 0), (hi, 32)):
                     c = moved[rel, at_row]
                     done += [c, send(base + 3, [c], CORE, out(rel, me, rows), out(rel, me, rows), piece, out(rel, ot, rows), **v)]
-            for way, rel, rows, at_row in () if direct else ((XP, 3, lo, 0), (XM, 1, hi, 32)):
+            for way, rel, rows, at_row in ((XP, 3, lo, 0), (XM, 1, hi, 32)):
                 c = send(base + 2, [moved[rel, at_row]], way, out(rel, me, rows), out(rel, me, rows), piece, out(2, me, rows), **v)
                 done += [c, send(base + 3, [c], CORE, out(2, me, rows), out(2, me, rows), piece, out(2, ot, rows), **v)]
             ready[h] = done
@@ -298,11 +249,11 @@
         return (value * r.slope[h, rows, :]).astype(BF)
 
     hidden = reduce_col(
-        lambda: r.T, tok, lambda: r.WI, load_in, 0, lambda: r.sum_h, lambda: r.H, finish_hidden, [load_bias_in], HALVES[0], DIRECT[0], 8)
+        lambda: r.T, tok, lambda: r.WI, load_in, 0, lambda: r.sum_h, lambda: r.H, finish_hidden, [load_bias_in], HALVES[0], 8)
     d_preact = reduce_col(
-        lambda: r.C, cot, lambda: r.WO, load_out, 1, lambda: r.sum_d, lambda: r.D, finish_d, [], HALVES[1], DIRECT[1], 12)
-
-    def reduce_row(total, ready, weight, dim, s, bias, also, target, brief, base):
+        lambda: r.C, cot, lambda: r.WO, load_out, 1, lambda: r.sum_d, lambda: r.D, finish_d, [], HALVES[1], 12)
+
+    def reduce_row(total, ready, weight, dim, s, bias, also, target, base):
         def product(q, n):
             def run():
                 left = total()[2 * q : 2 * q + 2].reshape(256, FW)
@@ -353,9 +304,12 @@
                                 szA, minor=0.001 * (4 - k), after=have(slot, A), run=run, cost=0.02 if run else 0.01)
                 ends.append(prev)
             own[s_] = task(base + 1, ends, have(0, A), run=add(0, (s_, full, A), (za, (0, 3, s_)), (za, (1, 3, s_))), cost=0.02)
-        y2 = send(base + 2, [], Y2, ref(0, 3, full, A), buf(ya, 2), szA, after=[own[3]])
-        p1 = send(base + 2, [], YP, ref(0, 1, full, A), buf(ya, 0), szA, after=[own[1]])
-        m1 = send(base + 2, [], YM, ref(0, 2, full, A), buf(ya, 1), szA, after=[own[2]])
+        p0 = send(base + 2, [], YP, ref(0, 3, lo, A), buf(ya, 0, 0, lo), szA // 2, after=[own[3]])
+        m0 = send(base + 2, [], YM, ref(0, 3, hi, A), buf(ya, 1, 0, hi), szA // 2, after=[own[3]])
+        p1 = send(base + 2, [p0], YP, ref(0, 1, full, A), buf(ya, 0, 1), szA, after=[own[1]],
+                  run=add(0, (1, lo, A), (ya, (0, 0, lo))), cost=0.02)
+        m1 = send(base + 2, [m0], YM, ref(0, 2, full, A), buf(ya, 1, 1), szA, after=[own[2]],
+                  run=add(0, (2, hi, A), (ya, (1, 0, hi))), cost=0.02)
         summed = {}
         for i, slot in enumerate(reversed(ARRIVAL)):
             z = POS[slot]
@@ -370,20 +324,9 @@
                                  after=here, run=run, cost=0.025 if run else 0.01, **v))
             summed[slot] = task(base + 3, ends, here, run=add(slot, (0, full, B), (yb, (0, 1, z)), (yb, (1, 1, z))), cost=0.03, **v)
         ends = []
-        for d, way, way2 in ((0, ZP, ZP2), (1, ZM, ZM2)):
+        for d, way in ((0, ZP), (1, ZM)):
             prev = None
             half = (lo, hi)[d]
-            if brief:
-                far, near, mid, end = (4, 3, 2, 1) if way == ZP else (4, 5, 6, 7)
-                b = base + 4
-                c0 = send(b, [], way2, ref(far, 0, half, B), buf(zb, d, 0, half), szB // 2, after=[summed[far]])
-                c1 = send(b, [], way, ref(near, 0, full, B), buf(zb, d, 1), szB, after=[summed[near]])
-                c3 = send(b, [], way, ref(end, 0, full, B), buf(zb, d, 3), szB, after=[summed[end]])
-                join = task(b, [c0, c1], [summed[mid]], run=add(mid, (0, full, B), (zb, (d, 1))), cost=0.02)
-                c2 = send(b, [c0, c1], way2, ref(mid, 0, full, B), buf(zb, d, 2), szB, after=[join],
-                          run=add(mid, (0, half, B), (zb, (d, 0, half))), cost=0.02)
-                ends += [c2, c3]
-                continue
             for k in range(4):
                 slot = 4 - k if way == ZP else (4 + k) % 8
                 rows, rows_in = (half if k == 0 else full), (half if k == 1 else full)
@@ -403,41 +346,42 @@
 
             return run
 
-        task(base + 2, [p1, m1, y2] + also, [own[0]], run=last(A, ya, (0, 1, 2)), cost=0.03)
-        task(base + 4, ends + also, [summed[0]], run=last(B, zb, ((0, 3), (1, 3), (0, 2), (1, 2)) if brief else ((0, 3), (1, 3))), cost=0.03)
-
-    reduce_row(lambda: r.H, hidden, lambda: r.WO, 0, lambda: r.sum_o, lambda: r.BO, [load_bias_out], lambda: r.outputs, BRIEF[0], 16)
-    reduce_row(lambda: r.D, d_preact, lambda: r.WI, 1, lambda: r.sum_t, None, [], lambda: r.d_tokens, BRIEF[1], 21)
+        task(base + 2, [p1, m1] + also, [own[0]], run=last(A, ya, ((0, 1), (1, 1))), cost=0.03)
+        task(base + 4, ends + also, [summed[0]], run=last(B, zb, ((0, 3), (1, 3))), cost=0.03)
+
+    reduce_row(lambda: r.H, hidden, lambda: r.WO, 0, lambda: r.sum_o, lambda: r.BO, [load_bias_out], lambda: r.outputs, 16)
+    reduce_row(lambda: r.D, d_preact, lambda: r.WI, 1, lambda: r.sum_t, None, [], lambda: r.d_tokens, 21)
 
     all_tok, all_cot = sum(tok, []), sum(cot, [])
 
-    def grad(left, right, target, i, wide):
+    def grad(left, right, target, i, n):
         def run():
-            cols = slice(i * 256, i * 256 + 256)
-            a = left()[..., cols].reshape(1024, 256)
-            target()[cols, :] = contract(a, right()[...].reshape(1024, wide), 0, 0).astype(BF)
+            rows, cols = slice(i * 256, i * 256 + 256), slice(n * FW, n * FW + FW)
+            a, b = left()[..., rows].reshape(1024, 256), right()[..., cols].reshape(1024, FW)
+            target()[rows, cols] = contract(a, b, 0, 0).astype(BF)
 
         return run
 
-    def column_sum(source, target):
+    def column_sum(source, target, n):
         def run():
-            whole = source()
-            lead, width = whole.shape[1], whole.shape[-1]
+            cols = slice(n * FW, n * FW + FW)
+            _, lead, rows, _ = source().shape
 
             def step(n, total):
-                return total + whole[n // lead, lax.rem(n, lead)].astype(F32)
-
-            total = lax.fori_loop(0, NZ * lead, step, jnp.zeros(whole.shape[2:], F32))
-            target()[...] = jnp.sum(total, axis=0, keepdims=True)
+                return total + source()[n // lead, lax.rem(n, lead), :, cols].astype(F32)
+
+            total = lax.fori_loop(0, NZ * lead, step, jnp.zeros((rows, FW), F32))
+            target()[:, cols] = jnp.sum(total, axis=0, keepdims=True)
 
         return run
 
-    for i in range(3):
-        task(26, all_cot + sum(hidden, []), run=grad(lambda: r.H, lambda: r.C, lambda: r.grad_w_out, i, DW), cost=0.95)
     for i in range(6):
-        task(26, all_tok + sum(d_preact, []), run=grad(lambda: r.T, lambda: r.D, lambda: r.grad_w_in, i, FW), cost=0.45)
-    task(27, all_cot, run=column_sum(lambda: r.C, lambda: r.grad_bias_out), cost=0.75)
-    task(27, sum(d_preact, []), run=column_sum(lambda: r.D, lambda: r.grad_bias_in), cost=0.4)
+        task(26, all_cot + sum(hidden, []), run=grad(lambda: r.H, lambda: r.C, lambda: r.grad_w_out, i // 2, i % 2), cost=0.5)
+    for i in range(6):
+        task(26, all_tok + sum(d_preact, []), run=grad(lambda: r.T, lambda: r.D, lambda: r.grad_w_in, i, 0), cost=0.45)
+    for n in range(2):
+        task(27, all_cot, run=column_sum(lambda: r.C, lambda: r.grad_bias_out, n), cost=0.4)
+    task(27, sum(d_preact, []), run=column_sum(lambda: r.D, lambda: r.grad_bias_in, 0), cost=0.4)
     return copies, tasks
 
 
@@ -446,10 +390,10 @@
         return pltpu.VMEM(shape, dtype)
 
     def col():
-        return dict(part=v(NZ, 2, CHUNK, FW), swap=v(NZ, CHUNK, FW), first=v(2, 2, 32, FW), second=v(2, 3, CHUNK, FW))
+        return dict(part=v(NZ, 2, CHUNK, FW), swap=v(NZ, CHUNK, FW), first=v(2, 2, 32, FW), second=v(2, 2, CHUNK, FW))
 
     def row():
-        return dict(part=v(NZ, NY, SHARD, DW), za=v(2, 4, NY, SHARD, CA), ya=v(3, SHARD, CA),
+        return dict(part=v(NZ, NY, SHARD, DW), za=v(2, 4, NY, SHARD, CA), ya=v(2, 2, SHARD, CA),
                     yb=v(2, 2, NZ, SHARD, CB), zb=v(2, 4, SHARD, CB))
 
     return dict(
@@ -474,8 +418,7 @@
         (lax.rem(z + 1, NZ) * NY + y, col), (lax.rem(z + NZ - 1, NZ) * NY + y, col),
         (z * NY + lax.rem(y + 1, NY), col), (z * NY + lax.rem(y + NY - 1, NY), col),
         (row, xs[1] * 2 + core), (row, xs[3] * 2 + core),
-        (lax.rem(z + 2, NZ) * NY + y, col), (lax.rem(z + NZ - 2, NZ) * NY + y, col),
-        (z * NY + lax.rem(y + 2, NY), col), (row, xs[2] * 2 + core), (row, x * 2 + other),
+        (row, x * 2 + other),
     )
     barrier = pltpu.get_barrier_semaphore()
     for target in to:
@@ -492,7 +435,7 @@
 
     copies, tasks = plan(r, at)
     waited = set()
-    for t in arrange(tasks):
+    for t in (tasks[i] for i in ORDER):
         for c in t.needs:
             if c.index not in waited:
                 waited.add(c.index)

time: 111 us -> 101 us (0.910); the launches traced: 111 us -> 99.2 us
  Pallas kernels: 110 us -> 98.4 us
    pallas_call x1, Pallas kernels: 108 us -> 96.1 us  [body(): pl.pallas_call(kernel, out_shape=tuple((pltpu.VMEM(shape, dtype) for shap...]
where the time goes in v2:
time: 101 us; the launch traced here: 99.2 us
  Pallas kernels  98.4 us (97%)
    pallas_call x1, Pallas kernels, body(): pl.pallas_call(kernel, out_shape=tuple((pltpu.VMEM(shape, dtype) for shap...  96.1 us
    pallas_call x1, Pallas kernels, body(): pl.pallas_call(store_kernel, out_shape=tuple((jax.ShapeDtypeStruct(shape...  2.31 us

profile of v2, /device:TPU:32, one launch (start us, length us, event | category | flops | bytes accessed | tf_op | source)
XLA Modules:
  0.0 99.2 jit_solution(7495991610536669271)
XLA Ops:
  0.6 96.1 %ffn.1 = (bf16[32,1536]{1,0:T(8,128)(2,1)S(1)}, bf16[32,1536]{1,0:T(8,128)(2,1)S(1)}, bf16[1536,768]{1,0:T(8,128)(2,1)S(1)}, f32[1,768]{1,0:T(1,128)S(1)}, bf16[...) custom-call(bf16[32,1536]{1,0:T(8,128)(2,1)} %tokens.1, bf16[1536,768]{1,0:T(8,128)(2,1)} %w_in.1, f32[768]{0:T(1024)} %bias_in.1, ...), custom_call_target="tpu_custom_call" | custom-call | flops 14495514624 | bytes 9437184 | tf_op jit(solution)/shard_map/ffn/pallas_call | solution.py:472
  96.8 2.3 %store.1 = (bf16[32,1536]{1,0:T(8,128)(2,1)}, bf16[32,1536]{1,0:T(8,128)(2,1)}, bf16[1536,768]{1,0:T(8,128)(2,1)}, f32[768]{0:T(1024)}, bf16[768,1536]{1,0:T(8,128)(2,1)}, /*index=5*/f32[1536]{0:T(1024)}) custom-call(bf16[32,1536]{1,0:T(8,128)(2,1)S(1)} %get-tuple-element.12.refs_0_, bf16[32,1536]{1,0:T(8,128)(2,1)S(1)} %get-tuple-element.13.refs_1_, ...), custom_call_target="tpu_custom_call" | custom-call | tf_op jit(solution)/shard_map/store/pallas_call | solution.py:486
